TPU v7x, 32 devices: a whole 2x2x4 slice. The times are simulated.
32 devices in a mesh: prow: 8 (over y, x, core), pcol: 4 (over z).
Axes of the slice: x: 2, y: 2, z: 4, core: 2. Of those that a mesh axis runs over, the one named last changes fastest.
Arguments:
- block: float32 [16384, 5120], P('prow', 'pcol'), may hold values from -6 to 6
Outputs:
- top: float32 [256, 5120], P(None, 'pcol')
- updated: float32 [16384, 5120], P('prow', 'pcol')
All inputs are finite; a program needn't handle non-finite values.
Results may differ from a plain program's by a relative error of at most 0.000073.
Values sent between devices are 32-bit elements; how exact they have to be, the bound alone decides.
A program may use at most 128 MiB of HBM per device.

v0:
```python
import jax
import jax.numpy as jnp
from jax import lax
from jax.sharding import PartitionSpec as P

NB = 256


def spread(value, axis, source):
    kept = jnp.where(lax.axis_index(axis) == source, value, 0).astype(value.dtype)
    return lax.psum(kept, axis)


def solve_triangular(matrix, right):
    return jax.scipy.linalg.solve_triangular(matrix, right, lower=True)


def inner(left, right):
    return jnp.dot(
        left.T, right, precision=lax.Precision.HIGHEST, preferred_element_type=jnp.float32
    )


def body(block):
    highest = lax.Precision.HIGHEST
    cols_here = block.shape[1]
    own_panel = block[:, :NB]
    gram = lax.psum(inner(own_panel, own_panel), "prow")
    factor = jnp.linalg.cholesky(gram)
    own_basis = solve_triangular(factor, own_panel.T).T
    basis = spread(own_basis, "pcol", 0)
    top = lax.psum(inner(basis, block), "prow")
    rest = block - jnp.dot(basis, top, precision=highest, preferred_element_type=jnp.float32)
    widened = jnp.pad(basis, ((0, 0), (0, cols_here - NB)))
    column_ids = lax.axis_index("pcol") * cols_here + jnp.arange(cols_here, dtype=jnp.int32)
    updated = jnp.where((column_ids < NB)[None, :], widened, rest)
    return (top, updated)


def solution(mesh):
    placed = (P("prow", "pcol"),)
    return jax.shard_map(
        body,
        mesh=mesh,
        in_specs=placed,
        out_specs=(P(None, "pcol"), P("prow", "pcol")),
        check_vma=False,
    )
```

profile of v0, /device:TPU:27, one launch (start us, length us, event | category | flops | bytes accessed | tf_op | source)
XLA Modules:
  0.0 323.9 jit_solution(10348194705665348174)
XLA Ops:
  7.2 0.0 all-reduce.6.cloned.1.call-start
  7.2 6.7 %fusion.1 = f32[256,256]{0,1:T(8,128)} fusion(f32[2048,1280]{1,0:T(8,128)} %param.1), kind=kOutput, calls=%fused_computation.7 | convolution fusion | flops 1610612736 | bytes 2359296 | tf_op jit(solution)/shard_map/dot_general | solution.py:19
  13.9 0.0 all-reduce.6.cloned.1.call-update
  13.9 0.2 all-reduce.8.cloned.1.call-start
  14.2 1.7 slice_bitcast_fusion
  15.9 50.9 %all-reduce.6.cloned.1.call-done = f32[256,256]{0,1:T(8,128)} async-done(((f32[256,256]{0,1:T(8,128)}), f32[256,256]{0,1:T(8,128)}) %all-reduce.6.cloned.1.call-update) | async-done | bytes 262160 | tf_op jit(solution)/shard_map/psum | solution.py:28
  66.9 1.1 copy.4
  67.9 1.0 fusion.5
  69.0 11.7 %cholesky.50 = f32[128,128]{1,0:T(8,128)S(1)} custom-call(f32[128,128]{1,0:T(8,128)S(1)} %cholesky.118), custom_call_target="Cholesky" | custom-call | tf_op jit(solution)/shard_map/jit(cholesky)/cholesky | solution.py:29
  80.7 9.8 %custom-call.15 = f32[1,128,128]{1,2,0:T(8,128)S(1)} custom-call(f32[1,128,128]{2,1,0:T(8,128)S(1)} %get-tuple-element.25), custom_call_target="InvertDiagBlocksLowerTriangular" | custom-call | tf_op jit(solution)/shard_map/jit(cholesky)/cholesky | solution.py:29
  90.5 0.2 constant_dynamic-update-slice_fusion.1
  90.8 0.3 convolution_subtract_fusion.1
  91.0 11.7 %cholesky.105 = f32[128,128]{1,0:T(8,128)S(1)} custom-call(f32[128,128]{1,0:T(8,128)S(1)} %convolution_subtract_fusion.1), custom_call_target="Cholesky" | custom-call | tf_op jit(solution)/shard_map/jit(cholesky)/cholesky | solution.py:29
  102.8 0.7 compare_reduce_fusion
  104.9 0.1 triangular_solve.57
  105.0 4.3 %while.1 = (s32[]{:T(128)}, f32[256,256]{1,0:T(8,128)S(1)}, s32[2,2]{1,0:T(2,128)S(1)}, f32[2,128,128]{2,1,0:T(8,128)S(1)}, s32[]{:T(128)}) while((s32[]{:T(128)}, f32[256,256]{1,0:T(8,128)S(1)}, s32[2,2]{1,0:T(2,128)S(1)}, f32[2,128,128]{2,1,0:T(8,128)S(1)}, s32[]{:T(128)}) %tuple.28), condition=%wide.while_cond, body=%wide.while_body.sunk | while | flops 2 | bytes 131189 | solution.py:15
  105.1 0.6 fusion.22
  105.7 1.4 bitcast_dynamic-update-slice_fusion.2
  107.2 0.6 fusion.22
  107.8 1.4 bitcast_dynamic-update-slice_fusion.2
  109.2 19.7 %custom-call.16 = f32[2,128,128]{1,2,0:T(8,128)S(1)} custom-call(f32[2,128,128]{2,1,0:T(8,128)S(1)} %get-tuple-element.9), custom_call_target="InvertDiagBlocksLowerTriangular" | custom-call | tf_op jit(solution)/shard_map/jit(_solve_triangular)/triangular_solve | solution.py:15
  128.9 1.1 fusion.3
  130.0 1.8 convolution_subtract_fusion
  131.8 1.1 fusion.7
  132.9 1.5 fusion
  134.4 0.0 all-reduce.8.cloned.1.call-update
  134.4 0.0 all-reduce.10.cloned.1.call-start
  134.5 85.9 %all-reduce.8.cloned.1.call-done = f32[2048,256]{0,1:T(8,128)} async-done(((f32[2048,256]{0,1:T(8,128)}), f32[2048,256]{0,1:T(8,128)}) %all-reduce.8.cloned.1.call-update) | async-done | bytes 2097168 | tf_op jit(solution)/shard_map/psum | solution.py:11
  220.4 13.0 %fusion.12 = f32[256,1280]{1,0:T(8,128)} fusion(f32[2048,256]{0,1:T(8,128)} %all-reduce.8.cloned.1.call-done, f32[2048,1280]{1,0:T(8,128)} %param.1), kind=kOutput, calls=%fused_computation.35 | convolution fusion | flops 8053063680 | bytes 13893632 | tf_op jit(solution)/shard_map/dot_general | solution.py:19
  233.4 0.0 all-reduce.10.cloned.1.call-update
  233.4 0.0 copy-start
  233.4 11.4 %copy.5 = f32[2048,1280]{0,1:T(8,128)} copy(f32[2048,1280]{1,0:T(8,128)} %param.1) | data formatting | bytes 20971520 | tf_op args[0]
  244.9 45.1 %all-reduce.10.cloned.1.call-done = f32[256,1280]{1,0:T(8,128)} async-done(((f32[256,1280]{1,0:T(8,128)}), f32[256,1280]{1,0:T(8,128)}) %all-reduce.10.cloned.1.call-update) | async-done | bytes 1310736 | tf_op jit(solution)/shard_map/psum | solution.py:32
  289.9 0.0 copy-done
  289.9 15.0 %subtract_select_fusion = f32[2048,1280]{0,1:T(8,128)} fusion(f32[2048,1280]{0,1:T(8,128)} %copy.5, f32[2048,256]{0,1:T(8,128)S(1)} %copy-done, f32[256,1280]{1,0:T(8,128)} %all-reduce.10.cloned.1.call-done, pred[1280]{0:T(1024)(128)(4,1)S(1)} %add_compare_fusion), kind=kOutput, calls=%fused_computation.2 | convolution fusion | flops 8058306560 | bytes 24380672 | tf_op jit(solution)/shard_map/dot_general | solution.py:33
  304.9 0.0 copy-start.1
  304.9 11.3 %copy.7 = f32[2048,1280]{1,0:T(8,128)} copy(f32[2048,1280]{0,1:T(8,128)} %subtract_select_fusion) | data formatting | bytes 20971520
  316.3 0.0 copy-done.1
  316.3 1.1 copy.23
  (10 shorter events, 0.2 us)
Async XLA Ops:
  7.2 59.7 %all-reduce.6.cloned.1.call-start = ((), (), s32[]{:S(2)}) async-start(), calls=%async_computation | async-start | bytes 524288 | tf_op jit(solution)/shard_map/psum | solution.py:28
  13.9 206.5 %all-reduce.8.cloned.1.call-start = ((), (), s32[]{:S(2)}) async-start(), calls=%async_computation.1 | async-start | bytes 4194304 | tf_op jit(solution)/shard_map/psum | solution.py:11
  134.4 155.5 %all-reduce.10.cloned.1.call-start = ((), (), s32[]{:S(2)}) async-start(), calls=%async_computation.2 | async-start | bytes 2621440 | tf_op jit(solution)/shard_map/psum | solution.py:32
  233.4 56.5 %copy-start = (f32[2048,256]{0,1:T(8,128)S(1)}, f32[2048,256]{0,1:T(8,128)}, u32[]{:S(2)}) copy-start(f32[2048,256]{0,1:T(8,128)} %all-reduce.8.cloned.1.call-done) | copy-start | bytes 6291460
  304.9 11.3 %copy-start.1 = (f32[256,1280]{1,0:T(8,128)S(1)}, f32[256,1280]{1,0:T(8,128)}, u32[]{:S(2)}) copy-start(f32[256,1280]{1,0:T(8,128)} %all-reduce.10.cloned.1.call-done) | copy-start | bytes 3932164
Sparse Core Ops, SparseCore 0:
  14.1 52.7 all-reduce.5
  134.5 85.8 all-reduce.7
  233.5 56.3 all-reduce.9
where the time goes:
time: 328 us; the launch traced here: 324 us
  waiting for transfers between devices  182 us (55%)
  other arithmetic  56.2 us (17%)
  matrix products  39.1 us (12%)
  local copies, waits for them, and re-layouts  30.8 us (9%)
  between operations  15.2 us (5%)
    psum x1, waiting for transfers between devices, spread(): return lax.psum(kept, axis)  85.9 us
    psum x1, waiting for transfers between devices, body(): gram = lax.psum(inner(own_panel, own_panel), 'prow')  50.9 us
    psum x1, waiting for transfers between devices, body(): top = lax.psum(inner(basis, block), 'prow')  45.1 us
    another operation x6, other arithmetic, body(): factor = jnp.linalg.cholesky(gram)  34 us
    unnamed x7, local copies, waits for them, and re-layouts  23.8 us
    another operation x3, other arithmetic, solve_triangular(): return jax.scipy.linalg.solve_triangular(matrix, right, lower=True)  19.7 us
    dot_general x2, matrix products, inner(): jnp.dot(left.T, right, precision=lax.Precision.HIGHEST, preferred_element...  19.7 us
    dot_general x1, matrix products, body(): jnp.dot(basis, top, precision=highest, preferred_element_type=jnp.float32)  15 us
  transfers between devices with their start and end apart: 3, of which 3 were waited for; matrix products, arithmetic and copies ran while one was open for 4% of the time, Pallas kernels for 0%

commit v1 on v0

v1 whole, which is shorter than its diff:
```python
import functools

import jax
import jax.numpy as jnp
from jax import lax
from jax.experimental import pallas as pl
from jax.experimental.pallas import tpu as pltpu
from jax.sharding import PartitionSpec as P

NB = 256
HALF = 128
ROWS = 256
DIAG = 64
HIGHEST = lax.Precision.HIGHEST
F32 = jnp.float32


def split(x):
    hi = x.astype(jnp.bfloat16)
    return hi, (x - hi.astype(F32)).astype(jnp.bfloat16)


def dot3(a, b):
    dot = functools.partial(jnp.dot, preferred_element_type=F32)
    return dot(a[0], b[0]) + (dot(a[0], b[1]) + dot(a[1], b[0]))


def inverse_factor(square):
    n = square.shape[0]
    row_id = lax.broadcasted_iota(jnp.int32, (n, 1), 0)
    eye = (
        lax.broadcasted_iota(jnp.int32, (n, n), 0)
        == lax.broadcasted_iota(jnp.int32, (n, n), 1)
    ).astype(F32)
    m = jnp.concatenate([square, eye], axis=1)
    for k in range(n - 1):
        row = m[k : k + 1, :]
        scaled = row / row[:, k : k + 1]
        m = m - jnp.where(row_id > k, m[:, k : k + 1], 0.0) * scaled
    pivots = jnp.sum(m[:, :n] * eye, axis=1, keepdims=True)
    return m[:, n:] / jnp.sqrt(pivots)


def inverse_cholesky(work):
    for start in range(0, NB, DIAG):
        end = start + DIAG
        inv = inverse_factor(work[start:end, start:end])
        new = jnp.dot(inv, work[start:end, :], precision=HIGHEST, preferred_element_type=F32)
        work[start:end, :] = new
        if end < NB:
            turned = new[:, :NB].T
            work[end:, :] = work[end:, :] - jnp.dot(
                turned[end:, :], new, precision=HIGHEST, preferred_element_type=F32
            )


def gather_kernel(
    np_, nq, block, panel_out, linv_out, prod_out,
    blk, panel, acc, parts, prod, gram, gparts, gfull, work, linv,
    load_sem, blk_sem, csend, crecv, gsend, grecv, hsend, hrecv,
    psend, precv, asend, arecv, zsend, zrecv, lsend, lrecv, out_sem,
):
    p = lax.axis_index("prow")
    q = lax.axis_index("pcol")
    rows, cols = blk.shape
    steps = rows // ROWS
    chunks = 2 * steps
    first = q == 0
    inner = q > 0
    sends_on = q < nq - 1
    gs = NB // np_
    ps = HALF // np_

    def remote(src, dst, send, recv, pp, qq):
        return pltpu.make_async_remote_copy(
            src_ref=src, dst_ref=dst, send_sem=send, recv_sem=recv,
            device_id={"prow": pp, "pcol": qq}, device_id_type=pl.DeviceIdType.MESH,
        )

    def peer(d):
        return lax.rem(p + d, np_)

    def load(h, r):
        at = pl.ds(r * ROWS, ROWS)
        return pltpu.make_async_copy(
            block.at[at, pl.ds(h * HALF, HALF)], panel.at[h, at], load_sem.at[h * steps + r]
        )

    def load_blk(r):
        at = pl.ds(r * ROWS, ROWS)
        return pltpu.make_async_copy(block.at[at], blk.at[at], blk_sem.at[r])

    def pass_on(h, r):
        at = pl.ds(r * ROWS, ROWS)
        c = h * steps + r
        return remote(panel.at[h, at], panel.at[h, at], csend.at[c], crecv.at[c], p, q + 1)

    def gram_part(d):
        j = peer(d)
        return remote(
            gram.at[pl.ds(pl.multiple_of(j * gs, 8), gs)], gparts.at[p],
            gsend.at[d], grecv.at[p], j, q,
        )

    def gram_wait(d):
        j = peer(d)
        return remote(
            gram.at[pl.ds(0, gs)], gparts.at[j], gsend.at[d], grecv.at[j], j, q
        )

    def spread_rows(ref, size, send, recv, d):
        at = pl.ds(pl.multiple_of(p * size, 8), size)
        return remote(ref.at[at], ref.at[at], send.at[d], recv.at[p], peer(d), q)

    def spread_wait(ref, size, send, recv, d):
        j = peer(d)
        at = pl.ds(pl.multiple_of(j * size, 8), size)
        return remote(ref.at[at], ref.at[at], send.at[d], recv.at[j], j, q)

    def prod_part(h, d):
        j = peer(d)
        return remote(
            acc.at[h, pl.ds(pl.multiple_of(j * ps, 8), ps)], parts.at[h, p],
            psend.at[h, d], precv.at[h, p], j, q,
        )

    def prod_wait(h, d):
        j = peer(d)
        return remote(
            acc.at[h, pl.ds(0, ps)], parts.at[h, j], psend.at[h, d], precv.at[h, j], j, q
        )

    own_l = pl.ds(pl.multiple_of(p * gs, 8), gs)

    def linv_on():
        return remote(linv.at[own_l], linv.at[own_l], zsend, zrecv, p, q + 1)

    @pl.when(first)
    def _():
        for h in range(2):
            for r in range(steps):
                load(h, r).start()

    for r in range(steps):
        load_blk(r).start()

    barrier = pltpu.get_barrier_semaphore()
    for d in range(1, np_):
        pl.semaphore_signal(
            barrier, inc=1, device_id={"prow": peer(d), "pcol": q},
            device_id_type=pl.DeviceIdType.MESH,
        )

    @pl.when(inner)
    def _():
        pl.semaphore_signal(
            barrier, inc=1, device_id={"prow": p, "pcol": q - 1},
            device_id_type=pl.DeviceIdType.MESH,
        )

    @pl.when(sends_on)
    def _():
        pl.semaphore_signal(
            barrier, inc=1, device_id={"prow": p, "pcol": q + 1},
            device_id_type=pl.DeviceIdType.MESH,
        )

    pl.semaphore_wait(
        barrier, np_ - 1 + jnp.where(inner, 1, 0) + jnp.where(sends_on, 1, 0)
    )

    @pl.when(first)
    def _():
        for h in range(2):
            for r in range(steps):
                load(h, r).wait()
                if nq > 1:
                    pass_on(h, r).start()
        gram[...] = jnp.zeros_like(gram)

        @pl.loop(0, steps)
        def _(r):
            at = pl.ds(pl.multiple_of(r * ROWS, ROWS), ROWS)
            both = jnp.concatenate([panel[0, at, :], panel[1, at, :]], axis=1)
            gram[...] += jnp.dot(both.T, both, precision=HIGHEST, preferred_element_type=F32)

        for d in range(1, np_):
            gram_part(d).start()
        total = gram[own_l, :]
        for d in range(1, np_):
            gram_wait(d).wait_recv()
            total = total + gparts[peer(d)]
        gfull[own_l, :] = total
        for d in range(1, np_):
            spread_rows(gfull, gs, hsend, hrecv, d).start()
        for d in range(1, np_):
            spread_wait(gfull, gs, hsend, hrecv, d).wait_recv()
        work[:, :NB] = gfull[...]
        work[:, NB:] = (
            lax.broadcasted_iota(jnp.int32, (NB, NB), 0)
            == lax.broadcasted_iota(jnp.int32, (NB, NB), 1)
        ).astype(F32)
        inverse_cholesky(work)
        linv[...] = work[:, NB:]
        if nq > 1:
            linv_on().start()
        for d in range(1, np_):
            gram_part(d).wait_send()
            spread_rows(gfull, gs, hsend, hrecv, d).wait_send()

    acc[...] = jnp.zeros_like(acc)

    def reduce_start(h):
        for d in range(1, np_):
            prod_part(h, d).start()

    def reduce_end(h):
        own = pl.ds(pl.multiple_of(p * ps, 8), ps)
        total = acc[h, own, :]
        for d in range(1, np_):
            prod_wait(h, d).wait_recv()
            total = total + parts[h, peer(d)]
        prod[h, own, :] = total
        for d in range(1, np_):
            spread_rows(prod.at[h], ps, asend.at[h], arecv.at[h], d).start()

    for h in range(2):

        @pl.loop(0, steps)
        def _(r):
            at = pl.ds(pl.multiple_of(r * ROWS, ROWS), ROWS)

            @pl.when(inner)
            def _():
                pass_on(h, r).wait_recv()

            @pl.when(jnp.logical_and(inner, sends_on))
            def _():
                pass_on(h, r).start()

            if h == 0:
                load_blk(r).wait()
            left = split(panel[h, at, :].T)
            for c in range(0, cols, 256):
                right = split(blk[at, c : c + 256])
                acc[h, :, c : c + 256] += dot3(left, right)

            if h == 1:

                @pl.when(r == steps // 2)
                def _():
                    reduce_end(0)

        reduce_start(h)

    panel_copy = pltpu.make_async_copy(panel, panel_out, out_sem.at[0])
    panel_copy.start()

    @pl.when(inner)
    def _():
        linv_on().wait_recv()

        @pl.when(sends_on)
        def _():
            linv_on().start()

        for d in range(1, np_):
            spread_rows(linv, gs, lsend, lrecv, d).start()

    reduce_end(1)

    @pl.when(inner)
    def _():
        for d in range(1, np_):
            spread_wait(linv, gs, lsend, lrecv, d).wait_recv()

    linv_copy = pltpu.make_async_copy(linv, linv_out, out_sem.at[1])
    linv_copy.start()
    for h in range(2):
        for d in range(1, np_):
            spread_wait(prod.at[h], ps, asend.at[h], arecv.at[h], d).wait_recv()
    prod_copy = pltpu.make_async_copy(prod, prod_out, out_sem.at[2])
    prod_copy.start()

    for h in range(2):
        for d in range(1, np_):
            prod_part(h, d).wait_send()
            spread_rows(prod.at[h], ps, asend.at[h], arecv.at[h], d).wait_send()

    @pl.when(inner)
    def _():
        for d in range(1, np_):
            spread_rows(linv, gs, lsend, lrecv, d).wait_send()

    @pl.when(sends_on)
    def _():
        for h in range(2):
            for r in range(steps):
                pass_on(h, r).wait_send()
        linv_on().wait_send()

    panel_copy.wait()
    linv_copy.wait()
    prod_copy.wait()


def update_kernel(block, panel, linv, prod, top, updated, left_inv, right_top):
    cols = block.shape[1]

    @pl.when(pl.program_id(0) == 0)
    def _():
        for c in range(0, cols, 256):
            at = slice(c, c + 256)
            products = jnp.concatenate([prod[0, :, at], prod[1, :, at]], axis=0)
            tile = jnp.dot(linv[...], products, precision=HIGHEST, preferred_element_type=F32)
            top[:, at] = tile
            right_top[0, :, at], right_top[1, :, at] = split(tile)
        left_inv[0], left_inv[1] = split(linv[...].T)

    both = jnp.concatenate([panel[0], panel[1]], axis=1)
    basis = dot3(split(both), (left_inv[0], left_inv[1]))
    left = split(basis)
    for c in range(0, cols, 256):
        at = slice(c, c + 256)
        right = (right_top[0, :, at], right_top[1, :, at])
        updated[:, at] = block[:, at] - dot3(left, right)

    @pl.when(lax.axis_index("pcol") == 0)
    def _():
        updated[:, :NB] = basis


def body(np_, nq, block):
    rows, cols = block.shape
    steps = rows // ROWS
    gs = NB // np_
    ps = HALF // np_
    dma = pltpu.SemaphoreType.DMA
    hbm = pl.BlockSpec(memory_space=pl.ANY)
    flops = 3 * 2 * rows * NB * cols
    panel, linv, prod = pl.pallas_call(
        functools.partial(gather_kernel, np_, nq),
        out_shape=(
            jax.ShapeDtypeStruct((2, rows, HALF), F32),
            jax.ShapeDtypeStruct((NB, NB), F32),
            jax.ShapeDtypeStruct((2, HALF, cols), F32),
        ),
        in_specs=[hbm],
        out_specs=(hbm, hbm, hbm),
        scratch_shapes=[
            pltpu.VMEM((rows, cols), F32),
            pltpu.VMEM((2, rows, HALF), F32),
            pltpu.VMEM((2, HALF, cols), F32),
            pltpu.VMEM((2, np_, ps, cols), F32),
            pltpu.VMEM((2, HALF, cols), F32),
            pltpu.VMEM((NB, NB), F32),
            pltpu.VMEM((np_, gs, NB), F32),
            pltpu.VMEM((NB, NB), F32),
            pltpu.VMEM((NB, 2 * NB), F32),
            pltpu.VMEM((NB, NB), F32),
            dma((2 * steps,)),
            dma((steps,)),
            dma((2 * steps,)),
            dma((2 * steps,)),
            dma((np_,)),
            dma((np_,)),
            dma((np_,)),
            dma((np_,)),
            dma((2, np_)),
            dma((2, np_)),
            dma((2, np_)),
            dma((2, np_)),
            dma,
            dma,
            dma((np_,)),
            dma((np_,)),
            dma((3,)),
        ],
        compiler_params=pltpu.CompilerParams(
            collective_id=0, has_side_effects=True, vmem_limit_bytes=32 * 2**20
        ),
        cost_estimate=pl.CostEstimate(
            flops=flops, bytes_accessed=4 * rows * cols, transcendentals=0
        ),
    )(block)
    whole = lambda *shape: pl.BlockSpec(shape, lambda i: (0,) * len(shape))
    return pl.pallas_call(
        update_kernel,
        grid=(steps,),
        out_shape=(
            jax.ShapeDtypeStruct((NB, cols), F32),
            jax.ShapeDtypeStruct((rows, cols), F32),
        ),
        in_specs=[
            pl.BlockSpec((ROWS, cols), lambda i: (i, 0)),
            pl.BlockSpec((2, ROWS, HALF), lambda i: (0, i, 0)),
            whole(NB, NB),
            whole(2, HALF, cols),
        ],
        out_specs=(whole(NB, cols), pl.BlockSpec((ROWS, cols), lambda i: (i, 0))),
        scratch_shapes=[
            pltpu.VMEM((2, NB, NB), jnp.bfloat16),
            pltpu.VMEM((2, NB, cols), jnp.bfloat16),
        ],
        compiler_params=pltpu.CompilerParams(vmem_limit_bytes=32 * 2**20),
        cost_estimate=pl.CostEstimate(
            flops=flops, bytes_accessed=8 * rows * cols, transcendentals=0
        ),
    )(block, panel, linv, prod)


def solution(mesh):
    return jax.shard_map(
        functools.partial(body, mesh.shape["prow"], mesh.shape["pcol"]),
        mesh=mesh,
        in_specs=(P("prow", "pcol"),),
        out_specs=(P(None, "pcol"), P("prow", "pcol")),
        check_vma=False,
    )
```

time: 328 us -> 95.8 us (0.29)
  the two profiles are of different devices: /device:TPU:27 before, /device:TPU:1 now
where the time goes in v1:
time: 95.8 us; the launch traced here: 95.6 us
  Pallas kernels  91 us (95%)
  local copies, waits for them, and re-layouts  3.97 us (4%)
    pallas_call x1, Pallas kernels, body(): pl.pallas_call(functools.partial(gather_kernel, np_, nq), out_shape=(jax....  79.5 us
    pallas_call x1, Pallas kernels, body(): pl.pallas_call(update_kernel, grid=(steps,), out_shape=(jax.ShapeDtypeStr...  11.5 us
    unnamed x2, local copies, waits for them, and re-layouts  3.97 us

profile of v1, /device:TPU:1, one launch (start us, length us, event | category | flops | bytes accessed | tf_op | source)
XLA Modules:
  0.0 95.6 jit_solution(12728168770306264059)
XLA Ops:
  0.6 0.0 copy-start
  0.6 4.0 %copy-done = f32[2048,1280]{1,0:T(8,128)S(1)} copy-done((f32[2048,1280]{1,0:T(8,128)S(1)}, f32[2048,1280]{1,0:T(8,128)}, u32[]{:S(2)}) %copy-start) | copy-done | bytes 10485784
  4.6 79.5 %shard_map.30 = (f32[2,2048,128]{2,1,0:T(8,128)S(1)}, f32[256,256]{1,0:T(8,128)S(1)}, f32[2,128,1280]{2,1,0:T(8,128)S(1)}) custom-call(f32[2048,1280]{1,0:T(8,128)S(1)} %copy-done), custom_call_target="tpu_custom_call" | custom-call | flops 4026531840 | bytes 10485760 | tf_op jit(solution)/shard_map/pallas_call | solution.py:341
  84.1 11.5 %shard_map.31 = (f32[256,1280]{1,0:T(8,128)}, f32[2048,1280]{1,0:T(8,128)}) custom-call(f32[2048,1280]{1,0:T(8,128)S(1)} %copy-done, f32[2,2048,128]{2,1,0:T(8,128)S(1)} %get-tuple-element.5.panel, f32[256,256]{1,0:T(8,128)S(1)} %get-tuple-element.6.linv, f32[2,128,1280]{2,1,0:T(8,128)S(1)} %get-tuple-element.7.prod), custom_call_target="tpu_custom_call" | custom-call | flops 4026531840 | bytes 20971520 | tf_op jit(solution)/shard_map/pallas_call | solution.py:387
Async XLA Ops:
  0.6 4.0 %copy-start = (f32[2048,1280]{1,0:T(8,128)S(1)}, f32[2048,1280]{1,0:T(8,128)}, u32[]{:S(2)}) copy-start(f32[2048,1280]{1,0:T(8,128)} %block.3) | copy-start | bytes 31457284

commit v2 on v1

--- a/solution.py
+++ b/solution.py
@@ -10,6 +10,7 @@
 NB = 256
 HALF = 128
 ROWS = 256
+PIECE = 128
 DIAG = 64
 HIGHEST = lax.Precision.HIGHEST
 F32 = jnp.float32
@@ -20,38 +21,63 @@
     return hi, (x - hi.astype(F32)).astype(jnp.bfloat16)
 
 
+def left_terms(x):
+    hi, lo = split(x)
+    return jnp.concatenate([hi, lo, hi], axis=1)
+
+
+def right_terms(x):
+    hi, lo = split(x)
+    return jnp.concatenate([hi, hi, lo], axis=0)
+
+
 def dot3(a, b):
-    dot = functools.partial(jnp.dot, preferred_element_type=F32)
-    return dot(a[0], b[0]) + (dot(a[0], b[1]) + dot(a[1], b[0]))
+    return jnp.dot(a, b, preferred_element_type=F32)
 
 
 def inverse_factor(square):
     n = square.shape[0]
-    row_id = lax.broadcasted_iota(jnp.int32, (n, 1), 0)
+    below = lax.broadcasted_iota(jnp.int32, (8, 1), 0)
     eye = (
         lax.broadcasted_iota(jnp.int32, (n, n), 0)
         == lax.broadcasted_iota(jnp.int32, (n, n), 1)
     ).astype(F32)
-    m = jnp.concatenate([square, eye], axis=1)
-    for k in range(n - 1):
-        row = m[k : k + 1, :]
-        scaled = row / row[:, k : k + 1]
-        m = m - jnp.where(row_id > k, m[:, k : k + 1], 0.0) * scaled
+    rest = jnp.concatenate([square, eye], axis=1)
+    done = []
+    for g in range(0, n, 8):
+        cols = [jnp.broadcast_to(rest[:, k : k + 1], rest.shape) for k in range(g, g + 8)]
+        head, rest = rest[:8], rest[8:]
+        for j in range(8):
+            inv = 1.0 / cols[j][j : j + 1, :]
+            row = head[j : j + 1, :] * inv
+            if j < 7:
+                head = head - jnp.where(below > j, cols[j][:8], 0.0) * row
+            if g + 8 < n:
+                rest = rest - cols[j][8:] * row
+            for i in range(j + 1, 8):
+                cols[i] = cols[i] - cols[j] * (cols[i][j : j + 1, :] * inv)
+        done.append(head)
+    m = jnp.concatenate(done, axis=0)
     pivots = jnp.sum(m[:, :n] * eye, axis=1, keepdims=True)
     return m[:, n:] / jnp.sqrt(pivots)
 
 
 def inverse_cholesky(work):
-    for start in range(0, NB, DIAG):
-        end = start + DIAG
-        inv = inverse_factor(work[start:end, start:end])
-        new = jnp.dot(inv, work[start:end, :], precision=HIGHEST, preferred_element_type=F32)
-        work[start:end, :] = new
-        if end < NB:
-            turned = new[:, :NB].T
-            work[end:, :] = work[end:, :] - jnp.dot(
-                turned[end:, :], new, precision=HIGHEST, preferred_element_type=F32
-            )
+    row_id = lax.broadcasted_iota(jnp.int32, (NB, 1), 0)
+
+    @pl.loop(0, NB // DIAG)
+    def _(b):
+        at = pl.ds(pl.multiple_of(b * DIAG, DIAG), DIAG)
+        band = work[at, :]
+        square = band[:, :DIAG]
+        for other in range(1, NB // DIAG):
+            square = jnp.where(b == other, band[:, other * DIAG : (other + 1) * DIAG], square)
+        new = jnp.dot(
+            inverse_factor(square), band, precision=HIGHEST, preferred_element_type=F32
+        )
+        lower = jnp.where(row_id >= (b + 1) * DIAG, new[:, :NB].T, 0.0)
+        work[...] -= jnp.dot(lower, new, precision=HIGHEST, preferred_element_type=F32)
+        work[at, :] = new
 
 
 def gather_kernel(
@@ -64,7 +90,8 @@
     q = lax.axis_index("pcol")
     rows, cols = blk.shape
     steps = rows // ROWS
-    chunks = 2 * steps
+    pieces = rows // PIECE
+    per_step = ROWS // PIECE
     first = q == 0
     inner = q > 0
     sends_on = q < nq - 1
@@ -81,9 +108,9 @@
         return lax.rem(p + d, np_)
 
     def load(h, r):
-        at = pl.ds(r * ROWS, ROWS)
+        at = pl.ds(r * PIECE, PIECE)
         return pltpu.make_async_copy(
-            block.at[at, pl.ds(h * HALF, HALF)], panel.at[h, at], load_sem.at[h * steps + r]
+            block.at[at, pl.ds(h * HALF, HALF)], panel.at[h, at], load_sem.at[h * pieces + r]
         )
 
     def load_blk(r):
@@ -91,8 +118,8 @@
         return pltpu.make_async_copy(block.at[at], blk.at[at], blk_sem.at[r])
 
     def pass_on(h, r):
-        at = pl.ds(r * ROWS, ROWS)
-        c = h * steps + r
+        at = pl.ds(r * PIECE, PIECE)
+        c = h * pieces + r
         return remote(panel.at[h, at], panel.at[h, at], csend.at[c], crecv.at[c], p, q + 1)
 
     def gram_part(d):
@@ -138,7 +165,7 @@
     @pl.when(first)
     def _():
         for h in range(2):
-            for r in range(steps):
+            for r in range(pieces):
                 load(h, r).start()
 
     for r in range(steps):
@@ -172,7 +199,7 @@
     @pl.when(first)
     def _():
         for h in range(2):
-            for r in range(steps):
+            for r in range(pieces):
                 load(h, r).wait()
                 if nq > 1:
                     pass_on(h, r).start()
@@ -230,19 +257,21 @@
         def _(r):
             at = pl.ds(pl.multiple_of(r * ROWS, ROWS), ROWS)
 
-            @pl.when(inner)
-            def _():
-                pass_on(h, r).wait_recv()
-
-            @pl.when(jnp.logical_and(inner, sends_on))
-            def _():
-                pass_on(h, r).start()
+            for piece in range(per_step):
+
+                @pl.when(inner)
+                def _():
+                    pass_on(h, r * per_step + piece).wait_recv()
+
+                @pl.when(jnp.logical_and(inner, sends_on))
+                def _():
+                    pass_on(h, r * per_step + piece).start()
 
             if h == 0:
                 load_blk(r).wait()
-            left = split(panel[h, at, :].T)
+            left = left_terms(panel[h, at, :].T)
             for c in range(0, cols, 256):
-                right = split(blk[at, c : c + 256])
+                right = right_terms(blk[at, c : c + 256])
                 acc[h, :, c : c + 256] += dot3(left, right)
 
             if h == 1:
@@ -295,7 +324,7 @@
     @pl.when(sends_on)
     def _():
         for h in range(2):
-            for r in range(steps):
+            for r in range(pieces):
                 pass_on(h, r).wait_send()
         linv_on().wait_send()
 
@@ -304,7 +333,7 @@
     prod_copy.wait()
 
 
-def update_kernel(block, panel, linv, prod, top, updated, left_inv, right_top):
+def update_kernel(block, panel, linv, prod, top, updated, right_inv, right_top):
     cols = block.shape[1]
 
     @pl.when(pl.program_id(0) == 0)
@@ -314,16 +343,15 @@
             products = jnp.concatenate([prod[0, :, at], prod[1, :, at]], axis=0)
             tile = jnp.dot(linv[...], products, precision=HIGHEST, preferred_element_type=F32)
             top[:, at] = tile
-            right_top[0, :, at], right_top[1, :, at] = split(tile)
-        left_inv[0], left_inv[1] = split(linv[...].T)
+            right_top[:, at] = right_terms(tile)
+        right_inv[...] = right_terms(linv[...].T)
 
     both = jnp.concatenate([panel[0], panel[1]], axis=1)
-    basis = dot3(split(both), (left_inv[0], left_inv[1]))
-    left = split(basis)
+    basis = dot3(left_terms(both), right_inv[...])
+    left = left_terms(basis)
     for c in range(0, cols, 256):
         at = slice(c, c + 256)
-        right = (right_top[0, :, at], right_top[1, :, at])
-        updated[:, at] = block[:, at] - dot3(left, right)
+        updated[:, at] = block[:, at] - dot3(left, right_top[:, at])
 
     @pl.when(lax.axis_index("pcol") == 0)
     def _():
@@ -333,6 +361,7 @@
 def body(np_, nq, block):
     rows, cols = block.shape
     steps = rows // ROWS
+    pieces = rows // PIECE
     gs = NB // np_
     ps = HALF // np_
     dma = pltpu.SemaphoreType.DMA
@@ -358,10 +387,10 @@
             pltpu.VMEM((NB, NB), F32),
             pltpu.VMEM((NB, 2 * NB), F32),
             pltpu.VMEM((NB, NB), F32),
-            dma((2 * steps,)),
+            dma((2 * pieces,)),
             dma((steps,)),
-            dma((2 * steps,)),
-            dma((2 * steps,)),
+            dma((2 * pieces,)),
+            dma((2 * pieces,)),
             dma((np_,)),
             dma((np_,)),
             dma((np_,)),
@@ -377,7 +406,7 @@
             dma((3,)),
         ],
         compiler_params=pltpu.CompilerParams(
-            collective_id=0, has_side_effects=True, vmem_limit_bytes=32 * 2**20
+            collective_id=0, has_side_effects=True, vmem_limit_bytes=60 * 2**20
         ),
         cost_estimate=pl.CostEstimate(
             flops=flops, bytes_accessed=4 * rows * cols, transcendentals=0
@@ -399,10 +428,10 @@
         ],
         out_specs=(whole(NB, cols), pl.BlockSpec((ROWS, cols), lambda i: (i, 0))),
         scratch_shapes=[
-            pltpu.VMEM((2, NB, NB), jnp.bfloat16),
-            pltpu.VMEM((2, NB, cols), jnp.bfloat16),
+            pltpu.VMEM((3 * NB, NB), jnp.bfloat16),
+            pltpu.VMEM((3 * NB, cols), jnp.bfloat16),
         ],
-        compiler_params=pltpu.CompilerParams(vmem_limit_bytes=32 * 2**20),
+        compiler_params=pltpu.CompilerParams(vmem_limit_bytes=60 * 2**20),
         cost_estimate=pl.CostEstimate(
             flops=flops, bytes_accessed=8 * rows * cols, transcendentals=0
         ),

time: 95.8 us -> 92.7 us (0.968)
  the two profiles are of different devices: /device:TPU:1 before, /device:TPU:27 now
where the time goes in v2:
time: 92.7 us; the launch traced here: 92.1 us
  Pallas kernels  91.5 us (99%)
    pallas_call x1, Pallas kernels, body(): pl.pallas_call(functools.partial(gather_kernel, np_, nq), out_shape=(jax....  75.7 us
    pallas_call x1, Pallas kernels, body(): pl.pallas_call(update_kernel, grid=(steps,), out_shape=(jax.ShapeDtypeStr...  15.8 us

profile of v2, /device:TPU:27, one launch (start us, length us, event | category | flops | bytes accessed | tf_op | source)
XLA Modules:
  0.0 92.1 jit_solution(4821367659848527337)
XLA Ops:
  0.6 75.7 %shard_map.30 = (f32[2,2048,128]{2,1,0:T(8,128)}, f32[256,256]{1,0:T(8,128)}, f32[2,128,1280]{2,1,0:T(8,128)}) custom-call(f32[2048,1280]{1,0:T(8,128)} %block.3), custom_call_target="tpu_custom_call" | custom-call | flops 4026531840 | bytes 10485760 | tf_op jit(solution)/shard_map/pallas_call | solution.py:370
  76.3 15.8 %shard_map.31 = (f32[256,1280]{1,0:T(8,128)}, f32[2048,1280]{1,0:T(8,128)}) custom-call(f32[2048,1280]{1,0:T(8,128)} %block.3, f32[2,2048,128]{2,1,0:T(8,128)} %get-tuple-element.5.panel, f32[256,256]{1,0:T(8,128)} %get-tuple-element.6.linv, f32[2,128,1280]{2,1,0:T(8,128)} %get-tuple-element.7.prod), custom_call_target="tpu_custom_call" | custom-call | flops 4026531840 | bytes 20971520 | tf_op jit(solution)/shard_map/pallas_call | solution.py:416

commit v3 on v2

--- a/solution.py
+++ b/solution.py
@@ -92,6 +92,7 @@
     steps = rows // ROWS
     pieces = rows // PIECE
     per_step = ROWS // PIECE
+    ahead = pieces + pieces // 2
     first = q == 0
     inner = q > 0
     sends_on = q < nq - 1
@@ -201,7 +202,7 @@
         for h in range(2):
             for r in range(pieces):
                 load(h, r).wait()
-                if nq > 1:
+                if nq > 1 and h * pieces + r < ahead:
                     pass_on(h, r).start()
         gram[...] = jnp.zeros_like(gram)
 
@@ -231,6 +232,8 @@
         linv[...] = work[:, NB:]
         if nq > 1:
             linv_on().start()
+            for r in range(ahead - pieces, pieces):
+                pass_on(1, r).start()
         for d in range(1, np_):
             gram_part(d).wait_send()
             spread_rows(gfull, gs, hsend, hrecv, d).wait_send()
@@ -250,6 +253,18 @@
         prod[h, own, :] = total
         for d in range(1, np_):
             spread_rows(prod.at[h], ps, asend.at[h], arecv.at[h], d).start()
+
+    def linv_forward():
+        @pl.when(inner)
+        def _():
+            linv_on().wait_recv()
+
+            @pl.when(sends_on)
+            def _():
+                linv_on().start()
+
+            for d in range(1, np_):
+                spread_rows(linv, gs, lsend, lrecv, d).start()
 
     for h in range(2):
 
@@ -279,22 +294,12 @@
                 @pl.when(r == steps // 2)
                 def _():
                     reduce_end(0)
+                    linv_forward()
 
         reduce_start(h)
 
     panel_copy = pltpu.make_async_copy(panel, panel_out, out_sem.at[0])
     panel_copy.start()
-
-    @pl.when(inner)
-    def _():
-        linv_on().wait_recv()
-
-        @pl.when(sends_on)
-        def _():
-            linv_on().start()
-
-        for d in range(1, np_):
-            spread_rows(linv, gs, lsend, lrecv, d).start()
 
     reduce_end(1)
 
@@ -333,29 +338,31 @@
     prod_copy.wait()
 
 
-def update_kernel(block, panel, linv, prod, top, updated, right_inv, right_top):
-    cols = block.shape[1]
-
-    @pl.when(pl.program_id(0) == 0)
-    def _():
-        for c in range(0, cols, 256):
-            at = slice(c, c + 256)
-            products = jnp.concatenate([prod[0, :, at], prod[1, :, at]], axis=0)
-            tile = jnp.dot(linv[...], products, precision=HIGHEST, preferred_element_type=F32)
-            top[:, at] = tile
-            right_top[:, at] = right_terms(tile)
-        right_inv[...] = right_terms(linv[...].T)
-
-    both = jnp.concatenate([panel[0], panel[1]], axis=1)
-    basis = dot3(left_terms(both), right_inv[...])
-    left = left_terms(basis)
-    for c in range(0, cols, 256):
-        at = slice(c, c + 256)
-        updated[:, at] = block[:, at] - dot3(left, right_top[:, at])
-
-    @pl.when(lax.axis_index("pcol") == 0)
-    def _():
-        updated[:, :NB] = basis
+def update_kernel(block, panel, linv, prod, top, updated, basis, left, right_top):
+    i, c = pl.program_id(0), pl.program_id(1)
+
+    @pl.when(c == 0)
+    def _():
+        both = jnp.concatenate([panel[0], panel[1]], axis=1)
+        basis[...] = dot3(left_terms(both), right_terms(linv[...].T))
+        left[...] = left_terms(basis[...])
+
+    @pl.when(i == 0)
+    def _():
+        products = jnp.concatenate([prod[0], prod[1]], axis=0)
+        tile = jnp.dot(linv[...], products, precision=HIGHEST, preferred_element_type=F32)
+        top[...] = tile
+        right_top[c] = right_terms(tile)
+
+    in_panel = jnp.logical_and(c == 0, lax.axis_index("pcol") == 0)
+
+    @pl.when(in_panel)
+    def _():
+        updated[...] = basis[...]
+
+    @pl.when(jnp.logical_not(in_panel))
+    def _():
+        updated[...] = block[...] - dot3(left[...], right_top[c])
 
 
 def body(np_, nq, block):
@@ -412,24 +419,28 @@
             flops=flops, bytes_accessed=4 * rows * cols, transcendentals=0
         ),
     )(block)
-    whole = lambda *shape: pl.BlockSpec(shape, lambda i: (0,) * len(shape))
+    tall, tiles = rows // 2, cols // NB
     return pl.pallas_call(
         update_kernel,
-        grid=(steps,),
+        grid=(rows // tall, tiles),
         out_shape=(
             jax.ShapeDtypeStruct((NB, cols), F32),
             jax.ShapeDtypeStruct((rows, cols), F32),
         ),
         in_specs=[
-            pl.BlockSpec((ROWS, cols), lambda i: (i, 0)),
-            pl.BlockSpec((2, ROWS, HALF), lambda i: (0, i, 0)),
-            whole(NB, NB),
-            whole(2, HALF, cols),
+            pl.BlockSpec((tall, NB), lambda i, c: (i, c)),
+            pl.BlockSpec((2, tall, HALF), lambda i, c: (0, i, 0)),
+            pl.BlockSpec((NB, NB), lambda i, c: (0, 0)),
+            pl.BlockSpec((2, HALF, NB), lambda i, c: (0, 0, jnp.where(i == 0, c, tiles - 1))),
         ],
-        out_specs=(whole(NB, cols), pl.BlockSpec((ROWS, cols), lambda i: (i, 0))),
+        out_specs=(
+            pl.BlockSpec((NB, NB), lambda i, c: (0, jnp.where(i == 0, c, tiles - 1))),
+            pl.BlockSpec((tall, NB), lambda i, c: (i, c)),
+        ),
         scratch_shapes=[
-            pltpu.VMEM((3 * NB, NB), jnp.bfloat16),
-            pltpu.VMEM((3 * NB, cols), jnp.bfloat16),
+            pltpu.VMEM((tall, NB), F32),
+            pltpu.VMEM((tall, 3 * NB), jnp.bfloat16),
+            pltpu.VMEM((tiles, 3 * NB, NB), jnp.bfloat16),
         ],
         compiler_params=pltpu.CompilerParams(vmem_limit_bytes=60 * 2**20),
         cost_estimate=pl.CostEstimate(

time: 92.7 us -> 93.7 us (1.011)
  Pallas kernels: 91.5 us -> 92.7 us
where the time goes in v3:
time: 93.7 us; the launch traced here: 93.4 us
  Pallas kernels  92.7 us (99%)
    pallas_call x1, Pallas kernels, body(): pl.pallas_call(functools.partial(gather_kernel, np_, nq), out_shape=(jax....  76.5 us
    pallas_call x1, Pallas kernels, body(): pl.pallas_call(update_kernel, grid=(rows // tall, tiles), out_shape=(jax....  16.3 us

profile of v3, /device:TPU:27, one launch (start us, length us, event | category | flops | bytes accessed | tf_op | source)
XLA Modules:
  0.0 93.4 jit_solution(11301539751274736310)
XLA Ops:
  0.6 76.5 %shard_map.30 = (f32[2,2048,128]{2,1,0:T(8,128)}, f32[256,256]{1,0:T(8,128)}, f32[2,128,1280]{2,1,0:T(8,128)}) custom-call(f32[2048,1280]{1,0:T(8,128)} %block.3), custom_call_target="tpu_custom_call" | custom-call | flops 4026531840 | bytes 10485760 | tf_op jit(solution)/shard_map/pallas_call | solution.py:377
  77.1 16.3 %shard_map.31 = (f32[256,1280]{1,0:T(8,128)}, f32[2048,1280]{1,0:T(8,128)}) custom-call(f32[2048,1280]{1,0:T(8,128)} %block.3, f32[2,2048,128]{2,1,0:T(8,128)} %get-tuple-element.5.panel, f32[256,256]{1,0:T(8,128)} %get-tuple-element.6.linv, f32[2,128,1280]{2,1,0:T(8,128)} %get-tuple-element.7.prod), custom_call_target="tpu_custom_call" | custom-call | flops 4026531840 | bytes 20971520 | tf_op jit(solution)/shard_map/pallas_call | solution.py:423

commit v4 on v3

--- a/solution.py
+++ b/solution.py
@@ -81,8 +81,8 @@
 
 
 def gather_kernel(
-    np_, nq, block, panel_out, linv_out, prod_out,
-    blk, panel, acc, parts, prod, gram, gparts, gfull, work, linv,
+    np_, nq, block, blk, panel_out, linv_out, prod_out,
+    panel, acc, parts, prod, gram, gparts, gfull, work, linv,
     load_sem, blk_sem, csend, crecv, gsend, grecv, hsend, hrecv,
     psend, precv, asend, arecv, zsend, zrecv, lsend, lrecv, out_sem,
 ):
@@ -340,16 +340,19 @@
 
 def update_kernel(block, panel, linv, prod, top, updated, basis, left, right_top):
     i, c = pl.program_id(0), pl.program_id(1)
+    tall = updated.shape[0]
+    down = pl.ds(pl.multiple_of(i * tall, tall), tall)
+    across = pl.ds(pl.multiple_of(c * NB, NB), NB)
 
     @pl.when(c == 0)
     def _():
-        both = jnp.concatenate([panel[0], panel[1]], axis=1)
+        both = jnp.concatenate([panel[0, down, :], panel[1, down, :]], axis=1)
         basis[...] = dot3(left_terms(both), right_terms(linv[...].T))
         left[...] = left_terms(basis[...])
 
     @pl.when(i == 0)
     def _():
-        products = jnp.concatenate([prod[0], prod[1]], axis=0)
+        products = jnp.concatenate([prod[0, :, across], prod[1, :, across]], axis=0)
         tile = jnp.dot(linv[...], products, precision=HIGHEST, preferred_element_type=F32)
         top[...] = tile
         right_top[c] = right_terms(tile)
@@ -362,7 +365,7 @@
 
     @pl.when(jnp.logical_not(in_panel))
     def _():
-        updated[...] = block[...] - dot3(left[...], right_top[c])
+        updated[...] = block[down, across] - dot3(left[...], right_top[c])
 
 
 def body(np_, nq, block):
@@ -372,19 +375,19 @@
     gs = NB // np_
     ps = HALF // np_
     dma = pltpu.SemaphoreType.DMA
-    hbm = pl.BlockSpec(memory_space=pl.ANY)
+    vmem = pl.BlockSpec(memory_space=pltpu.VMEM)
     flops = 3 * 2 * rows * NB * cols
-    panel, linv, prod = pl.pallas_call(
+    block, panel, linv, prod = pl.pallas_call(
         functools.partial(gather_kernel, np_, nq),
         out_shape=(
-            jax.ShapeDtypeStruct((2, rows, HALF), F32),
-            jax.ShapeDtypeStruct((NB, NB), F32),
-            jax.ShapeDtypeStruct((2, HALF, cols), F32),
-        ),
-        in_specs=[hbm],
-        out_specs=(hbm, hbm, hbm),
+            pltpu.VMEM((rows, cols), F32),
+            pltpu.VMEM((2, rows, HALF), F32),
+            pltpu.VMEM((NB, NB), F32),
+            pltpu.VMEM((2, HALF, cols), F32),
+        ),
+        in_specs=[pl.BlockSpec(memory_space=pltpu.HBM)],
+        out_specs=(vmem,) * 4,
         scratch_shapes=[
-            pltpu.VMEM((rows, cols), F32),
             pltpu.VMEM((2, rows, HALF), F32),
             pltpu.VMEM((2, HALF, cols), F32),
             pltpu.VMEM((2, np_, ps, cols), F32),
@@ -413,7 +416,7 @@
             dma((3,)),
         ],
         compiler_params=pltpu.CompilerParams(
-            collective_id=0, has_side_effects=True, vmem_limit_bytes=60 * 2**20
+            collective_id=0, has_side_effects=True, vmem_limit_bytes=44 * 2**20
         ),
         cost_estimate=pl.CostEstimate(
             flops=flops, bytes_accessed=4 * rows * cols, transcendentals=0
@@ -427,12 +430,7 @@
             jax.ShapeDtypeStruct((NB, cols), F32),
             jax.ShapeDtypeStruct((rows, cols), F32),
         ),
-        in_specs=[
-            pl.BlockSpec((tall, NB), lambda i, c: (i, c)),
-            pl.BlockSpec((2, tall, HALF), lambda i, c: (0, i, 0)),
-            pl.BlockSpec((NB, NB), lambda i, c: (0, 0)),
-            pl.BlockSpec((2, HALF, NB), lambda i, c: (0, 0, jnp.where(i == 0, c, tiles - 1))),
-        ],
+        in_specs=[vmem] * 4,
         out_specs=(
             pl.BlockSpec((NB, NB), lambda i, c: (0, jnp.where(i == 0, c, tiles - 1))),
             pl.BlockSpec((tall, NB), lambda i, c: (i, c)),
@@ -442,7 +440,7 @@
             pltpu.VMEM((tall, 3 * NB), jnp.bfloat16),
             pltpu.VMEM((tiles, 3 * NB, NB), jnp.bfloat16),
         ],
-        compiler_params=pltpu.CompilerParams(vmem_limit_bytes=60 * 2**20),
+        compiler_params=pltpu.CompilerParams(vmem_limit_bytes=44 * 2**20),
         cost_estimate=pl.CostEstimate(
             flops=flops, bytes_accessed=8 * rows * cols, transcendentals=0
         ),

time: 93.7 us -> 95.6 us (1.020)
  local copies, waits for them, and re-layouts: 0 us -> 3.97 us
  Pallas kernels: 92.7 us -> 90.9 us
    unnamed x0 -> x2, local copies, waits for them, and re-layouts: none -> 3.97 us
    pallas_call x1, Pallas kernels: 16.3 us -> 15.3 us  [body(): pl.pallas_call(update_kernel, grid=(rows // tall, tiles), out_shape=(jax....]
where the time goes in v4:
time: 95.6 us; the launch traced here: 95.5 us
  Pallas kernels  90.9 us (95%)
  local copies, waits for them, and re-layouts  3.97 us (4%)
    pallas_call x1, Pallas kernels, body(): pl.pallas_call(functools.partial(gather_kernel, np_, nq), out_shape=(pltp...  75.6 us
    pallas_call x1, Pallas kernels, body(): pl.pallas_call(update_kernel, grid=(rows // tall, tiles), out_shape=(jax....  15.3 us
    unnamed x2, local copies, waits for them, and re-layouts  3.97 us

profile of v4, /device:TPU:27, one launch (start us, length us, event | category | flops | bytes accessed | tf_op | source)
XLA Modules:
  0.0 95.5 jit_solution(7764871195596208830)
XLA Ops:
  0.6 75.6 %shard_map.30 = (f32[2048,1280]{1,0:T(8,128)S(1)}, f32[2,2048,128]{2,1,0:T(8,128)S(1)}, f32[256,256]{1,0:T(8,128)S(1)}, f32[2,128,1280]{2,1,0:T(8,128)S(1)}) custom-call(f32[2048,1280]{1,0:T(8,128)} %block.1), custom_call_target="tpu_custom_call" | custom-call | flops 4026531840 | bytes 10485760 | tf_op jit(solution)/shard_map/pallas_call | solution.py:380
  76.2 0.0 copy-start
  76.2 4.0 %copy-done = f32[2048,1280]{1,0:T(8,128)} copy-done((f32[2048,1280]{1,0:T(8,128)}, f32[2048,1280]{1,0:T(8,128)S(1)}, u32[]{:S(2)}) %copy-start) | copy-done | bytes 10485784
  80.2 15.3 %shard_map.31 = (f32[256,1280]{1,0:T(8,128)}, f32[2048,1280]{1,0:T(8,128)}) custom-call(f32[2048,1280]{1,0:T(8,128)} %copy-done, f32[2,2048,128]{2,1,0:T(8,128)S(1)} %get-tuple-element.7.panel, f32[256,256]{1,0:T(8,128)S(1)} %get-tuple-element.8.linv, f32[2,128,1280]{2,1,0:T(8,128)S(1)} %get-tuple-element.9.prod), custom_call_target="tpu_custom_call" | custom-call | flops 4026531840 | bytes 20971520 | tf_op jit(solution)/shard_map/pallas_call | solution.py:426
Async XLA Ops:
  76.2 4.0 %copy-start = (f32[2048,1280]{1,0:T(8,128)}, f32[2048,1280]{1,0:T(8,128)S(1)}, u32[]{:S(2)}) copy-start(f32[2048,1280]{1,0:T(8,128)S(1)} %get-tuple-element.6.block) | copy-start | bytes 31457284

commit v5 on v4

--- a/solution.py
+++ b/solution.py
@@ -81,10 +81,10 @@
 
 
 def gather_kernel(
-    np_, nq, block, blk, panel_out, linv_out, prod_out,
-    panel, acc, parts, prod, gram, gparts, gfull, work, linv,
+    np_, nq, block, blk, panel, linv, prod,
+    acc, pair, parts, gram, gparts, gfull, work,
     load_sem, blk_sem, csend, crecv, gsend, grecv, hsend, hrecv,
-    psend, precv, asend, arecv, zsend, zrecv, lsend, lrecv, out_sem,
+    tsend, trecv, psend, precv, asend, arecv, bsend, brecv, zsend, zrecv, lsend, lrecv,
 ):
     p = lax.axis_index("prow")
     q = lax.axis_index("pcol")
@@ -98,6 +98,10 @@
     sends_on = q < nq - 1
     gs = NB // np_
     ps = HALF // np_
+    pairs = np_ // 2
+    parity, own_pair = lax.rem(p, 2), p // 2
+    sibling = p + 1 - 2 * parity
+    side = HALF // 2
 
     def remote(src, dst, send, recv, pp, qq):
         return pltpu.make_async_remote_copy(
@@ -145,18 +149,53 @@
         at = pl.ds(pl.multiple_of(j * size, 8), size)
         return remote(ref.at[at], ref.at[at], send.at[d], recv.at[j], j, q)
 
-    def prod_part(h, d):
-        j = peer(d)
+    def rows_of(par, m):
+        return pl.ds(pl.multiple_of(par * side + m * ps, 8), ps)
+
+    def pair_part(h):
+        theirs = pl.ds(pl.multiple_of((1 - parity) * side, 8), side)
+        return remote(acc.at[h, theirs], pair.at[h], tsend.at[h], trecv.at[h], sibling, q)
+
+    def other_pair(e):
+        return lax.rem(own_pair + e, pairs)
+
+    def prod_part(h, e):
+        m = other_pair(e)
         return remote(
-            acc.at[h, pl.ds(pl.multiple_of(j * ps, 8), ps)], parts.at[h, p],
-            psend.at[h, d], precv.at[h, p], j, q,
-        )
-
-    def prod_wait(h, d):
-        j = peer(d)
+            acc.at[h, rows_of(parity, m)], parts.at[h, own_pair],
+            psend.at[h, e], precv.at[h, own_pair], 2 * m + parity, q,
+        )
+
+    def prod_wait(h, e):
+        m = other_pair(e)
         return remote(
-            acc.at[h, pl.ds(0, ps)], parts.at[h, j], psend.at[h, d], precv.at[h, j], j, q
-        )
+            acc.at[h, rows_of(parity, m)], parts.at[h, m],
+            psend.at[h, e], precv.at[h, m], 2 * m + parity, q,
+        )
+
+    def sum_part(h, e):
+        m, at = other_pair(e), rows_of(parity, own_pair)
+        return remote(
+            prod.at[h, at], prod.at[h, at],
+            asend.at[h, e], arecv.at[h, own_pair], 2 * m + parity, q,
+        )
+
+    def sum_wait(h, e):
+        m = other_pair(e)
+        at = rows_of(parity, m)
+        return remote(
+            prod.at[h, at], prod.at[h, at], asend.at[h, e], arecv.at[h, m], 2 * m + parity, q
+        )
+
+    def across_part(h, e):
+        m = other_pair(e)
+        at = rows_of(parity, m)
+        return remote(prod.at[h, at], prod.at[h, at], bsend.at[h, e], brecv.at[h, m], sibling, q)
+
+    def across_wait(h, e):
+        m = other_pair(e)
+        at = rows_of(1 - parity, m)
+        return remote(prod.at[h, at], prod.at[h, at], bsend.at[h, e], brecv.at[h, m], sibling, q)
 
     own_l = pl.ds(pl.multiple_of(p * gs, 8), gs)
 
@@ -240,19 +279,28 @@
 
     acc[...] = jnp.zeros_like(acc)
 
-    def reduce_start(h):
-        for d in range(1, np_):
-            prod_part(h, d).start()
+    def reduce_middle(h):
+        pair_part(h).wait_recv()
+        mine = pl.ds(pl.multiple_of(parity * side, 8), side)
+        acc[h, mine, :] += pair[h]
+        for e in range(1, pairs):
+            prod_part(h, e).start()
 
     def reduce_end(h):
-        own = pl.ds(pl.multiple_of(p * ps, 8), ps)
+        own = rows_of(parity, own_pair)
         total = acc[h, own, :]
-        for d in range(1, np_):
-            prod_wait(h, d).wait_recv()
-            total = total + parts[h, peer(d)]
+        for e in range(1, pairs):
+            prod_wait(h, e).wait_recv()
+            total = total + parts[h, other_pair(e)]
         prod[h, own, :] = total
-        for d in range(1, np_):
-            spread_rows(prod.at[h], ps, asend.at[h], arecv.at[h], d).start()
+        for e in range(1, pairs):
+            sum_part(h, e).start()
+        across_part(h, 0).start()
+
+    def gather_across(h):
+        for e in range(1, pairs):
+            sum_wait(h, e).wait_recv()
+            across_part(h, e).start()
 
     def linv_forward():
         @pl.when(inner)
@@ -291,35 +339,41 @@
 
             if h == 1:
 
+                @pl.when(r == 1)
+                def _():
+                    reduce_middle(0)
+
                 @pl.when(r == steps // 2)
                 def _():
                     reduce_end(0)
                     linv_forward()
 
-        reduce_start(h)
-
-    panel_copy = pltpu.make_async_copy(panel, panel_out, out_sem.at[0])
-    panel_copy.start()
-
+                @pl.when(r == steps - 2)
+                def _():
+                    gather_across(0)
+
+        pair_part(h).start()
+
+    reduce_middle(1)
     reduce_end(1)
+    gather_across(1)
 
     @pl.when(inner)
     def _():
         for d in range(1, np_):
             spread_wait(linv, gs, lsend, lrecv, d).wait_recv()
 
-    linv_copy = pltpu.make_async_copy(linv, linv_out, out_sem.at[1])
-    linv_copy.start()
     for h in range(2):
-        for d in range(1, np_):
-            spread_wait(prod.at[h], ps, asend.at[h], arecv.at[h], d).wait_recv()
-    prod_copy = pltpu.make_async_copy(prod, prod_out, out_sem.at[2])
-    prod_copy.start()
+        for e in range(pairs):
+            across_wait(h, e).wait_recv()
 
     for h in range(2):
-        for d in range(1, np_):
-            prod_part(h, d).wait_send()
-            spread_rows(prod.at[h], ps, asend.at[h], arecv.at[h], d).wait_send()
+        pair_part(h).wait_send()
+        for e in range(pairs):
+            across_part(h, e).wait_send()
+        for e in range(1, pairs):
+            prod_part(h, e).wait_send()
+            sum_part(h, e).wait_send()
 
     @pl.when(inner)
     def _():
@@ -332,10 +386,6 @@
             for r in range(pieces):
                 pass_on(h, r).wait_send()
         linv_on().wait_send()
-
-    panel_copy.wait()
-    linv_copy.wait()
-    prod_copy.wait()
 
 
 def update_kernel(block, panel, linv, prod, top, updated, basis, left, right_top):
@@ -374,6 +424,7 @@
     pieces = rows // PIECE
     gs = NB // np_
     ps = HALF // np_
+    pairs = np_ // 2
     dma = pltpu.SemaphoreType.DMA
     vmem = pl.BlockSpec(memory_space=pltpu.VMEM)
     flops = 3 * 2 * rows * NB * cols
@@ -388,15 +439,13 @@
         in_specs=[pl.BlockSpec(memory_space=pltpu.HBM)],
         out_specs=(vmem,) * 4,
         scratch_shapes=[
-            pltpu.VMEM((2, rows, HALF), F32),
             pltpu.VMEM((2, HALF, cols), F32),
-            pltpu.VMEM((2, np_, ps, cols), F32),
-            pltpu.VMEM((2, HALF, cols), F32),
+            pltpu.VMEM((2, HALF // 2, cols), F32),
+            pltpu.VMEM((2, pairs, ps, cols), F32),
             pltpu.VMEM((NB, NB), F32),
             pltpu.VMEM((np_, gs, NB), F32),
             pltpu.VMEM((NB, NB), F32),
             pltpu.VMEM((NB, 2 * NB), F32),
-            pltpu.VMEM((NB, NB), F32),
             dma((2 * pieces,)),
             dma((steps,)),
             dma((2 * pieces,)),
@@ -405,15 +454,18 @@
             dma((np_,)),
             dma((np_,)),
             dma((np_,)),
-            dma((2, np_)),
-            dma((2, np_)),
-            dma((2, np_)),
-            dma((2, np_)),
+            dma((2,)),
+            dma((2,)),
+            dma((2, pairs)),
+            dma((2, pairs)),
+            dma((2, pairs)),
+            dma((2, pairs)),
+            dma((2, pairs)),
+            dma((2, pairs)),
             dma,
             dma,
             dma((np_,)),
             dma((np_,)),
-            dma((3,)),
         ],
         compiler_params=pltpu.CompilerParams(
             collective_id=0, has_side_effects=True, vmem_limit_bytes=44 * 2**20
@@ -440,7 +492,7 @@
             pltpu.VMEM((tall, 3 * NB), jnp.bfloat16),
             pltpu.VMEM((tiles, 3 * NB, NB), jnp.bfloat16),
         ],
-        compiler_params=pltpu.CompilerParams(vmem_limit_bytes=44 * 2**20),
+        compiler_params=pltpu.CompilerParams(vmem_limit_bytes=20 * 2**20),
         cost_estimate=pl.CostEstimate(
             flops=flops, bytes_accessed=8 * rows * cols, transcendentals=0
         ),

time: 95.6 us -> 84.1 us (0.88)
  Pallas kernels: 90.9 us -> 83.3 us
  local copies, waits for them, and re-layouts: 3.97 us -> 0 us
    unnamed x2 -> x0, local copies, waits for them, and re-layouts: 3.97 us -> none
    pallas_call x1, Pallas kernels: 15.3 us -> 11.3 us  [body(): pl.pallas_call(update_kernel, grid=(rows // tall, tiles), out_shape=(jax....]
    pallas_call x1, Pallas kernels: 75.6 us -> 72 us  [body(): pl.pallas_call(functools.partial(gather_kernel, np_, nq), out_shape=(pltp...]
where the time goes in v5:
time: 84.1 us; the launch traced here: 83.9 us
  Pallas kernels  83.3 us (99%)
    pallas_call x1, Pallas kernels, body(): pl.pallas_call(functools.partial(gather_kernel, np_, nq), out_shape=(pltp...  72 us
    pallas_call x1, Pallas kernels, body(): pl.pallas_call(update_kernel, grid=(rows // tall, tiles), out_shape=(jax....  11.3 us

profile of v5, /device:TPU:27, one launch (start us, length us, event | category | flops | bytes accessed | tf_op | source)
XLA Modules:
  0.0 83.9 jit_solution(9421451770627276014)
XLA Ops:
  0.6 72.0 %shard_map.30 = (f32[2048,1280]{1,0:T(8,128)S(1)}, f32[2,2048,128]{2,1,0:T(8,128)S(1)}, f32[256,256]{1,0:T(8,128)S(1)}, f32[2,128,1280]{2,1,0:T(8,128)S(1)}) custom-call(f32[2048,1280]{1,0:T(8,128)} %block.1), custom_call_target="tpu_custom_call" | custom-call | flops 4026531840 | bytes 10485760 | tf_op jit(solution)/shard_map/pallas_call | solution.py:431
  72.6 11.3 %shard_map.31 = (f32[256,1280]{1,0:T(8,128)}, f32[2048,1280]{1,0:T(8,128)}) custom-call(f32[2048,1280]{1,0:T(8,128)S(1)} %get-tuple-element.6.block, f32[2,2048,128]{2,1,0:T(8,128)S(1)} %get-tuple-element.7.panel, f32[256,256]{1,0:T(8,128)S(1)} %get-tuple-element.8.linv, f32[2,128,1280]{2,1,0:T(8,128)S(1)} %get-tuple-element.9.prod), custom_call_target="tpu_custom_call" | custom-call | flops 4026531840 | bytes 20971520 | tf_op jit(solution)/shard_map/pallas_call | solution.py:478

commit v6 on v5

--- a/solution.py
+++ b/solution.py
@@ -81,8 +81,8 @@
 
 
 def gather_kernel(
-    np_, nq, block, blk, panel, linv, prod,
-    acc, pair, parts, gram, gparts, gfull, work,
+    np_, nq, block, blk, basis, left_out, linv, prod,
+    panel, right_inv, acc, pair, parts, gram, gparts, gfull, work,
     load_sem, blk_sem, csend, crecv, gsend, grecv, hsend, hrecv,
     tsend, trecv, psend, precv, asend, arecv, bsend, brecv, zsend, zrecv, lsend, lrecv,
 ):
@@ -354,14 +354,28 @@
 
         pair_part(h).start()
 
+    @pl.when(inner)
+    def _():
+        for d in range(1, np_):
+            spread_wait(linv, gs, lsend, lrecv, d).wait_recv()
+
+    right_inv[...] = right_terms(linv[...].T)
+
+    def basis_rows(begin, end):
+        @pl.loop(begin, end)
+        def _(r):
+            at = pl.ds(pl.multiple_of(r * ROWS, ROWS), ROWS)
+            both = jnp.concatenate([panel[0, at, :], panel[1, at, :]], axis=1)
+            some = dot3(left_terms(both), right_inv[...])
+            basis[at, :] = some
+            left_out[at, :] = left_terms(some)
+
+    basis_rows(0, steps // 3)
     reduce_middle(1)
+    basis_rows(steps // 3, 2 * steps // 3)
     reduce_end(1)
+    basis_rows(2 * steps // 3, steps)
     gather_across(1)
-
-    @pl.when(inner)
-    def _():
-        for d in range(1, np_):
-            spread_wait(linv, gs, lsend, lrecv, d).wait_recv()
 
     for h in range(2):
         for e in range(pairs):
@@ -388,22 +402,20 @@
         linv_on().wait_send()
 
 
-def update_kernel(block, panel, linv, prod, top, updated, basis, left, right_top):
+def update_kernel(block, basis, left, linv, prod, top, updated, left_inv, right_top):
     i, c = pl.program_id(0), pl.program_id(1)
     tall = updated.shape[0]
     down = pl.ds(pl.multiple_of(i * tall, tall), tall)
     across = pl.ds(pl.multiple_of(c * NB, NB), NB)
 
-    @pl.when(c == 0)
-    def _():
-        both = jnp.concatenate([panel[0, down, :], panel[1, down, :]], axis=1)
-        basis[...] = dot3(left_terms(both), right_terms(linv[...].T))
-        left[...] = left_terms(basis[...])
+    @pl.when(jnp.logical_and(i == 0, c == 0))
+    def _():
+        left_inv[...] = left_terms(linv[...])
 
     @pl.when(i == 0)
     def _():
         products = jnp.concatenate([prod[0, :, across], prod[1, :, across]], axis=0)
-        tile = jnp.dot(linv[...], products, precision=HIGHEST, preferred_element_type=F32)
+        tile = dot3(left_inv[...], right_terms(products))
         top[...] = tile
         right_top[c] = right_terms(tile)
 
@@ -411,11 +423,11 @@
 
     @pl.when(in_panel)
     def _():
-        updated[...] = basis[...]
+        updated[...] = basis[down, :]
 
     @pl.when(jnp.logical_not(in_panel))
     def _():
-        updated[...] = block[down, across] - dot3(left[...], right_top[c])
+        updated[...] = block[down, across] - dot3(left[down, :], right_top[c])
 
 
 def body(np_, nq, block):
@@ -428,17 +440,20 @@
     dma = pltpu.SemaphoreType.DMA
     vmem = pl.BlockSpec(memory_space=pltpu.VMEM)
     flops = 3 * 2 * rows * NB * cols
-    block, panel, linv, prod = pl.pallas_call(
+    block, basis, left, linv, prod = pl.pallas_call(
         functools.partial(gather_kernel, np_, nq),
         out_shape=(
             pltpu.VMEM((rows, cols), F32),
-            pltpu.VMEM((2, rows, HALF), F32),
+            pltpu.VMEM((rows, NB), F32),
+            pltpu.VMEM((rows, 3 * NB), jnp.bfloat16),
             pltpu.VMEM((NB, NB), F32),
             pltpu.VMEM((2, HALF, cols), F32),
         ),
         in_specs=[pl.BlockSpec(memory_space=pltpu.HBM)],
-        out_specs=(vmem,) * 4,
+        out_specs=(vmem,) * 5,
         scratch_shapes=[
+            pltpu.VMEM((2, rows, HALF), F32),
+            pltpu.VMEM((3 * NB, NB), jnp.bfloat16),
             pltpu.VMEM((2, HALF, cols), F32),
             pltpu.VMEM((2, HALF // 2, cols), F32),
             pltpu.VMEM((2, pairs, ps, cols), F32),
@@ -482,21 +497,20 @@
             jax.ShapeDtypeStruct((NB, cols), F32),
             jax.ShapeDtypeStruct((rows, cols), F32),
         ),
-        in_specs=[vmem] * 4,
+        in_specs=[vmem] * 5,
         out_specs=(
             pl.BlockSpec((NB, NB), lambda i, c: (0, jnp.where(i == 0, c, tiles - 1))),
             pl.BlockSpec((tall, NB), lambda i, c: (i, c)),
         ),
         scratch_shapes=[
-            pltpu.VMEM((tall, NB), F32),
-            pltpu.VMEM((tall, 3 * NB), jnp.bfloat16),
+            pltpu.VMEM((NB, 3 * NB), jnp.bfloat16),
             pltpu.VMEM((tiles, 3 * NB, NB), jnp.bfloat16),
         ],
         compiler_params=pltpu.CompilerParams(vmem_limit_bytes=20 * 2**20),
         cost_estimate=pl.CostEstimate(
             flops=flops, bytes_accessed=8 * rows * cols, transcendentals=0
         ),
-    )(block, panel, linv, prod)
+    )(block, basis, left, linv, prod)
 
 
 def solution(mesh):

time: 84.1 us -> 83.1 us (0.988)
  Pallas kernels: 83.3 us -> 82.4 us
    pallas_call x1, Pallas kernels: 11.3 us -> 9.63 us  [body(): pl.pallas_call(update_kernel, grid=(rows // tall, tiles), out_shape=(jax....]
where the time goes in v6:
time: 83.1 us; the launch traced here: 83 us
  Pallas kernels  82.4 us (99%)
    pallas_call x1, Pallas kernels, body(): pl.pallas_call(functools.partial(gather_kernel, np_, nq), out_shape=(pltp...  72.7 us
    pallas_call x1, Pallas kernels, body(): pl.pallas_call(update_kernel, grid=(rows // tall, tiles), out_shape=(jax....  9.63 us

profile of v6, /device:TPU:27, one launch (start us, length us, event | category | flops | bytes accessed | tf_op | source)
XLA Modules:
  0.0 83.0 jit_solution(13874163606603367523)
XLA Ops:
  0.6 72.7 %shard_map.30 = (f32[2048,1280]{1,0:T(8,128)S(1)}, f32[2048,256]{1,0:T(8,128)S(1)}, bf16[2048,768]{1,0:T(8,128)(2,1)S(1)}, f32[256,256]{1,0:T(8,128)S(1)}, f32[2,128,1280]{2,1,0:T(8,128)S(1)}) custom-call(f32[2048,1280]{1,0:T(8,128)} %block.1), custom_call_target="tpu_custom_call" | custom-call | flops 4026531840 | bytes 10485760 | tf_op jit(solution)/shard_map/pallas_call | solution.py:443
  73.4 9.6 %shard_map.31 = (f32[256,1280]{1,0:T(8,128)}, f32[2048,1280]{1,0:T(8,128)}) custom-call(f32[2048,1280]{1,0:T(8,128)S(1)} %get-tuple-element.7.block, f32[2048,256]{1,0:T(8,128)S(1)} %get-tuple-element.8.basis, bf16[2048,768]{1,0:T(8,128)(2,1)S(1)} %get-tuple-element.9.left, f32[256,256]{1,0:T(8,128)S(1)} %get-tuple-element.10.linv, ...), custom_call_target="tpu_custom_call" | custom-call | flops 4026531840 | bytes 20971520 | tf_op jit(solution)/shard_map/pallas_call | solution.py:493

commit v7 on v6

--- a/solution.py
+++ b/solution.py
@@ -10,7 +10,7 @@
 NB = 256
 HALF = 128
 ROWS = 256
-PIECE = 128
+PIECE = 64
 DIAG = 64
 HIGHEST = lax.Precision.HIGHEST
 F32 = jnp.float32

time: 83.1 us -> 82.8 us (level)
  no operation moved by 1% of the time
where the time goes in v7:
time: 82.8 us; the launch traced here: 82.6 us
  Pallas kernels  82 us (99%)
    pallas_call x1, Pallas kernels, body(): pl.pallas_call(functools.partial(gather_kernel, np_, nq), out_shape=(pltp...  72.4 us
    pallas_call x1, Pallas kernels, body(): pl.pallas_call(update_kernel, grid=(rows // tall, tiles), out_shape=(jax....  9.63 us

profile of v7, /device:TPU:27, one launch (start us, length us, event | category | flops | bytes accessed | tf_op | source)
XLA Modules:
  0.0 82.6 jit_solution(17551279308150296982)
XLA Ops:
  0.6 72.4 %shard_map.30 = (f32[2048,1280]{1,0:T(8,128)S(1)}, f32[2048,256]{1,0:T(8,128)S(1)}, bf16[2048,768]{1,0:T(8,128)(2,1)S(1)}, f32[256,256]{1,0:T(8,128)S(1)}, f32[2,128,1280]{2,1,0:T(8,128)S(1)}) custom-call(f32[2048,1280]{1,0:T(8,128)} %block.1), custom_call_target="tpu_custom_call" | custom-call | flops 4026531840 | bytes 10485760 | tf_op jit(solution)/shard_map/pallas_call | solution.py:443
  73.0 9.6 %shard_map.31 = (f32[256,1280]{1,0:T(8,128)}, f32[2048,1280]{1,0:T(8,128)}) custom-call(f32[2048,1280]{1,0:T(8,128)S(1)} %get-tuple-element.7.block, f32[2048,256]{1,0:T(8,128)S(1)} %get-tuple-element.8.basis, bf16[2048,768]{1,0:T(8,128)(2,1)S(1)} %get-tuple-element.9.left, f32[256,256]{1,0:T(8,128)S(1)} %get-tuple-element.10.linv, ...), custom_call_target="tpu_custom_call" | custom-call | flops 4026531840 | bytes 20971520 | tf_op jit(solution)/shard_map/pallas_call | solution.py:493
